TPU v7x, 32 devices: a whole 2x2x4 slice. The times are simulated.
32 devices in a mesh: seq: 2 (over y), rep: 4 (over z), tensor: 4 (over x, core).
Axes of the slice: x: 2, y: 2, z: 4, core: 2. Of those that a mesh axis runs over, the one named last changes fastest.
Arguments:
- key_value_rows: bfloat16 [4, 3072, 8, 256], P('rep', ('seq', 'tensor')), may hold values from -32 to 32
- queries: bfloat16 [4, 64, 64, 128], P('rep', None, 'tensor'), may hold values from -136 to 136
- w_comp: bfloat16 [2048, 512], replicated, may hold values from -0.125 to 0.125
- latent_gain: bfloat16 [512], replicated, may hold values from 0.099609375 to 1.8984375
- w_up: bfloat16 [8, 512, 256], P('tensor'), may hold values from -0.25 to 0.25
- w_out: bfloat16 [8192, 8192], P('tensor', 'seq'), may hold values from -0.0625 to 0.0625
- replica_order: int32 [4], replicated, may hold values from 0 to 3, each once
Outputs:
- decoded: bfloat16 [4, 64, 8192], P('rep', None, 'seq')
Inputs may be any that keep to these rules, and one draw needn't show every extreme that they name: replica_order is a permutation of the prompts.
All inputs are finite; a program needn't handle non-finite values.
Results may differ from a plain program's by a relative error of at most 0.01.
Values may be sent and summed in bfloat16 or wider, within the bound.
No kernel may reach another device: no remote copies, remote signals or barrier semaphores. Data moves between devices by JAX's collectives and lax.ppermute only.
A program may use at most 64 MiB of HBM per device.

v0:
```python
import itertools
import math

import jax
import jax.numpy as jnp
from jax import lax
from jax.experimental import pallas as pl
from jax.experimental.pallas import tpu as pltpu
from jax.sharding import PartitionSpec as P

BF16, F32 = jnp.bfloat16, jnp.float32
MIB = 1024 * 1024
IN_VMEM = pl.BlockSpec(memory_space=pltpu.VMEM)
IN_SMEM = pl.BlockSpec(memory_space=pltpu.SMEM)
IN_HBM = pl.BlockSpec(memory_space=pltpu.HBM)
COPIES = 8


def shape(dims, dtype):
    return jax.ShapeDtypeStruct(dims, dtype)


def call(body, name, outs, operands, vmem, scratch=(), smem_in=0, smem_out=0, hbm_in=0, cost=None):
    kept = len(operands) - hbm_in
    specs = [IN_SMEM] * smem_in + [IN_VMEM] * (kept - smem_in) + [IN_HBM] * hbm_in
    operands = [
        *operands[:kept],
        *(pltpu.with_memory_space_constraint(operand, pltpu.HBM) for operand in operands[kept:]),
    ]
    out_specs = [IN_VMEM] * (len(outs) - smem_out) + [IN_SMEM] * smem_out
    return pl.pallas_call(
        body,
        out_shape=outs,
        in_specs=specs,
        out_specs=out_specs,
        scratch_shapes=list(scratch),
        compiler_params=pltpu.CompilerParams(vmem_limit_bytes=vmem * MIB),
        cost_estimate=cost,
        name=name,
    )(*operands)


def cost(flops, moved, exps=0):
    return pl.CostEstimate(flops=int(flops), bytes_accessed=int(moved), transcendentals=int(exps))


def dot(a, b):
    return jnp.dot(a, b, preferred_element_type=F32)


def compress(rows, weight, gain):
    projected = dot(rows, weight)
    scale = lax.rsqrt(jnp.mean(projected * projected, axis=-1, keepdims=True) + 1e-06)
    return (projected * scale * gain.astype(F32)[None]).astype(BF16)


def order_index(replica_order, orders):
    table = jnp.array(orders, jnp.int32)
    match = jnp.all(table == replica_order[None], axis=1)
    return jnp.sum(jnp.where(match, lax.iota(jnp.int32, len(orders)), 0))


def route_pairs(order, back):
    return [(p, r) if back else (r, p) for r, p in enumerate(order)]


def route(value, index, orders, back):
    def branch(order):
        return lambda v: lax.ppermute(v, "rep", route_pairs(order, back))

    return lax.switch(index, [branch(o) for o in orders], value)


def shift(value, axis, hops):
    size = lax.axis_size(axis)
    return lax.ppermute(value, axis, [(i, (i + hops) % size) for i in range(size)])


def swap(value, axis, bit):
    pairs = [(i, i ^ bit) for i in range(lax.axis_size(axis))]
    return lax.ppermute(value, axis, pairs)


def compress_kernel(chunks, *refs):
    (order_hbm, rows_hbm, weight_hbm, gain_hbm, query_hbm, latent_ref, half_ref, index_ref, pick_ref) = refs[:9]
    (order_ref, rows_ref, weight_ref, gain_ref, query_ref, wide, packed, sems) = refs[9:]
    tokens, groups, width = rows_ref.shape
    chunk = tokens // chunks
    copies = [pltpu.make_async_copy(order_hbm, order_ref, sems.at[0])]
    for i in range(chunks):
        at = pl.ds(i * chunk, chunk)
        copies.append(pltpu.make_async_copy(rows_hbm.at[0, at], rows_ref.at[at], sems.at[1 + i]))
    for group in range(groups):
        at = pl.ds(group * width, width)
        copies.append(
            pltpu.make_async_copy(weight_hbm.at[at], weight_ref.at[at], sems.at[1 + chunks + group])
        )
    copies.append(pltpu.make_async_copy(gain_hbm, gain_ref, sems.at[1 + chunks + groups]))
    copies.append(pltpu.make_async_copy(query_hbm.at[0], query_ref, sems.at[2 + chunks + groups]))
    for copy in copies:
        copy.start()

    copies[0].wait()
    count = order_ref.shape[0]
    here = lax.axis_index("rep")
    index, wanted, wanted_beside = 0, 0, 0
    for i in range(count):
        wanted = jnp.where(order_ref[i] == here, i, wanted)
        wanted_beside = jnp.where(order_ref[i] == (here ^ 1), i, wanted_beside)
        smaller = 0
        for j in range(i + 1, count):
            smaller = smaller + (order_ref[j] < order_ref[i]).astype(jnp.int32)
        index = index + smaller * math.factorial(count - 1 - i)
    index_ref[0] = index
    pick_ref[0] = (wanted_beside == (here ^ 2)).astype(jnp.int32)
    pick_ref[1] = jnp.where(wanted == here, 0, jnp.where(wanted == (here ^ 2), 1, 2))

    lanes = wide.shape[2]
    for i in range(chunks):
        copies[1 + i].wait()
        at = slice(i * chunk * groups, (i + 1) * chunk * groups)
        for part in range(wide.shape[0]):
            values = rows_ref[i * chunk : (i + 1) * chunk, :, part * lanes : (part + 1) * lanes]
            wide[part, at] = values.astype(F32).reshape(chunk * groups, lanes)
        for group in range(groups):
            for part in range(wide.shape[0]):
                start = group * width + part * lanes
                picked = wide[part, pl.ds(at.start + group, chunk, stride=groups), :]
                packed[i * chunk : (i + 1) * chunk, start : start + lanes] = picked.astype(BF16)
    for group in range(groups):
        copies[1 + chunks + group].wait()
    copies[1 + chunks + groups].wait()
    gain = gain_ref[...].astype(F32)[None]
    projected = dot(packed[...], weight_ref[...])
    scale = lax.rsqrt(jnp.mean(projected * projected, axis=-1, keepdims=True) + 1e-06)
    latent_ref[...] = (projected * scale * gain).astype(BF16)

    copies[2 + chunks + groups].wait()
    new_count, heads, head_size = query_ref.shape
    query = query_ref[...].astype(F32)
    upper = lax.axis_index("seq") == 1
    query = jnp.where(upper, query[:, heads // 2 :], query[:, : heads // 2])
    half_ref[...] = query.reshape(half_ref.shape).astype(BF16)


def score_kernel(parts, *refs):
    latent_refs, (lift_ref, query_ref), (score_ref, value_ref, top_ref) = (
        refs[:parts],
        refs[parts : parts + 2],
        refs[parts + 2 :],
    )
    head_size = query_ref.shape[-1]
    lift = lift_ref[lax.axis_index("seq")]
    query = query_ref[...]
    top = None
    for part, latent_ref in enumerate(latent_refs):
        tokens = latent_ref.shape[0]
        at = slice(part * tokens, (part + 1) * tokens)
        lifted = dot(latent_ref[...], lift).astype(BF16)
        score = lax.dot_general(
            lifted[:, :head_size], query, (((1,), (1,)), ((), ())), preferred_element_type=F32
        )
        score_ref[at] = score
        value_ref[at] = lifted[:, head_size:]
        part_top = jnp.max(score, axis=0, keepdims=True)
        top = part_top if top is None else jnp.maximum(top, part_top)
    top_ref[...] = jnp.broadcast_to(top, top_ref.shape)


def fetch_kernel(weight_ref, own_ref, sent_ref, kept_ref, sems):
    core = lax.axis_index("tensor") % 2
    depth, columns = sent_ref.shape
    rows = depth // COPIES
    group = lax.axis_index("seq")
    copies = []
    for part, (held_ref, half, first) in enumerate(
        ((own_ref, group, 0), (sent_ref, 1 - group, 1 - core), (kept_ref, 1 - group, core))
    ):
        first = pl.multiple_of(first * columns, columns)
        for i in range(COPIES):
            start = pl.multiple_of(half * depth + i * rows, rows)
            source = weight_ref.at[pl.ds(start, rows), pl.ds(first, held_ref.shape[1])]
            target = held_ref.at[pl.ds(i * rows, rows)]
            copies.append(pltpu.make_async_copy(source, target, sems.at[part, i]))
    for copy in copies:
        copy.start()
    for copy in copies:
        copy.wait()


def fetch(weight):
    depth, columns = weight.shape[0] // 2, weight.shape[1]
    return call(
        fetch_kernel,
        "fetch",
        [pltpu.VMEM((depth, width), weight.dtype) for width in (columns, columns // 2, columns // 2)],
        [weight],
        4,
        scratch=[pltpu.SemaphoreType.DMA((3, COPIES))],
        hbm_in=1,
        cost=cost(0, 0),
    )


def choose(pick, refs, out_ref):
    for i, ref in enumerate(refs):

        @pl.when(pick == i)
        def _():
            out_ref[...] = ref[...]


def pass_kernel(pick_ref, own_ref, second_ref, out_ref):
    choose(pick_ref[0], (own_ref, second_ref), out_ref)


def halve_kernel(near_ref, far_ref, upper_ref, lower_ref):
    half = upper_ref.shape[0]
    upper_ref[...] = near_ref[:half]
    lower_ref[...] = far_ref[half:]


def choose_and_score_kernel(parts, pick_ref, *refs):
    *refs, score_ref, value_ref, top_ref, query_ref = refs
    choose(pick_ref[1], refs[parts + 1 :], query_ref)
    score_kernel(parts, *refs[: parts + 1], query_ref, score_ref, value_ref, top_ref)


def score_call(name, latents, lift, query, pick=None):
    queries = [query] if pick is None else query
    tokens = sum(latent.shape[0] for latent in latents)
    rows, head_size = queries[0].shape
    outs = [shape((tokens, rows), F32), shape((tokens, head_size), BF16), shape((8, rows), F32)]
    operands = [*latents, lift, *queries]
    estimate = cost(0, 0)
    if pick is None:
        body = lambda *refs: score_kernel(len(latents), *refs)
        return call(body, name, outs, operands, 16, cost=estimate)
    body = lambda *refs: choose_and_score_kernel(len(latents), *refs)
    outs.append(shape((rows, head_size), BF16))
    return call(body, name, outs, [pick, *operands], 16, smem_in=1, cost=estimate)


def attend_kernel(block, *refs):
    (*score_refs, out_ref, turned) = refs
    new_count = out_ref.shape[0]
    triples = [score_refs[i : i + 3] for i in range(0, len(score_refs), 3)]
    head_size = triples[0][1].shape[-1]
    coef = head_size ** (-0.5) * math.log2(math.e)
    top = triples[0][2][:1]
    for triple in triples[1:]:
        top = jnp.maximum(top, triple[2][:1])
    total = jnp.zeros_like(top)
    summed = jnp.zeros((head_size, top.shape[1]), F32)
    for score_ref, value_ref, _ in triples:
        for start in range(0, score_ref.shape[0], block):
            at = slice(start, start + block)
            expo = jnp.exp2((score_ref[at] - top) * coef)
            total += jnp.sum(expo, axis=0, keepdims=True)
            summed += lax.dot_general(
                value_ref[at], expo.astype(BF16), (((0,), (0,)), ((), ())), preferred_element_type=F32
            )
    turned[...] = (summed / total).T
    heads = turned.shape[0] // new_count
    for head in range(heads):
        out_ref[:, head * head_size : (head + 1) * head_size] = turned[
            pl.ds(head, new_count, stride=heads), :
        ].astype(BF16)


def project_kernel(tile, rows_ref, weight_ref, out_ref):
    rows = rows_ref[...]
    width = out_ref.shape[2]
    for part in range(out_ref.shape[0]):
        for column in range(0, width, tile):
            at = part * width + column
            out_ref[part, :, column : column + tile] = dot(
                rows, weight_ref[:, at : at + tile]
            )


def project_more_kernel(tile, own, kept, rows_ref, weight_ref, before_ref, out_ref):
    here = lax.axis_index("tensor")
    core, chip = here % 2, here // 2
    half = core if own else 1 - core
    width = out_ref.shape[1]
    start = (chip if kept else 1 - chip) * width
    rows = rows_ref[...]
    for column in range(0, width, tile):
        at = pl.ds(pl.multiple_of(start + column, tile), tile)
        out_ref[:, column : column + tile] = before_ref[half, :, at] + dot(rows, weight_ref[:, at])


def add_kernel(one_ref, other_ref, out_ref):
    out_ref[...] = one_ref[...] + other_ref[...]


def sum_kernel(own_ref, beside_ref, across_ref, out_ref):
    out_ref[...] = (own_ref[...] + beside_ref[...] + across_ref[...]).astype(out_ref.dtype)


def join_kernel(places, *refs):
    pieces = refs[: len(places)]
    out_ref, sems = refs[-2:]
    here = lax.axis_index("tensor")
    core, chip = here % 2, here // 2
    width = pieces[0].shape[1]
    copies = []
    for i, place in enumerate(places):
        at = 2 * (1 - core if place // 2 else core) + (1 - chip if place % 2 else chip)
        at = pl.ds(pl.multiple_of(at * width, width), width)
        copies.append(pltpu.make_async_copy(pieces[i], out_ref.at[0, :, at], sems.at[i]))
    for copy in copies:
        copy.start()
    for copy in copies:
        copy.wait()


def join(places, pieces, before):
    new_count, width = pieces[0].shape
    return pl.pallas_call(
        lambda *refs: join_kernel(places, *refs),
        out_shape=shape((1, new_count, 4 * width), BF16),
        in_specs=[IN_VMEM] * len(places) + ([] if before is None else [IN_HBM]),
        out_specs=IN_HBM,
        scratch_shapes=[pltpu.SemaphoreType.DMA((len(places),))],
        input_output_aliases={} if before is None else {len(places): 0},
        compiler_params=pltpu.CompilerParams(vmem_limit_bytes=4 * MIB),
        name="join",
    )(*pieces, *([] if before is None else [before]))


def square_shards(key_value_rows, queries, w_comp, latent_gain, w_up, w_out, replica_order):
    orders = list(itertools.permutations(range(lax.axis_size("rep"))))
    _, new_count, heads, head_size = queries.shape
    _, tokens, all_groups, width = key_value_rows.shape
    latent_width = w_comp.shape[1]
    rows = heads // 2 * new_count

    chunks = 3 if tokens % 48 == 0 else 1
    latent, query, index, pick = call(
        lambda *refs: compress_kernel(chunks, *refs),
        "compress",
        [shape((tokens, latent_width), BF16), shape((rows, head_size), BF16), *[shape((n,), jnp.int32) for n in (1, 2)]],
        [replica_order, key_value_rows, w_comp, latent_gain, queries],
        16,
        scratch=[
            pltpu.SMEM(replica_order.shape, jnp.int32),
            pltpu.VMEM(key_value_rows.shape[1:], BF16),
            pltpu.VMEM(w_comp.shape, BF16),
            pltpu.VMEM(latent_gain.shape, BF16),
            pltpu.VMEM(queries.shape[1:], BF16),
            pltpu.VMEM((width // 128, tokens * all_groups, 128), F32),
            pltpu.VMEM((tokens, all_groups * width), BF16),
            pltpu.SemaphoreType.DMA((3 + chunks + all_groups,)),
        ],
        hbm_in=5,
        smem_out=2,
        cost=cost(0, 0),
    )

    near = swap(latent, "seq", 1)
    far = swap(latent, "tensor", 2)
    second_query = swap(query, "rep", 2)
    held, held_sent, held_kept = fetch(w_out)
    second_query, held = lax.optimization_barrier((second_query, held))
    (passed,) = call(
        pass_kernel,
        "pass",
        [shape(query.shape, query.dtype)],
        [pick, query, second_query],
        4,
        smem_in=1,
        cost=cost(0, 0),
    )
    near, far, _ = lax.optimization_barrier((near, far, passed))
    upper, lower = call(
        halve_kernel,
        "halve",
        [shape((tokens // 2, latent_width), BF16)] * 2,
        [near, far],
        4,
        cost=cost(0, 0),
    )
    corner = [swap(upper, "tensor", 2), swap(lower, "seq", 1)]
    passed = swap(passed, "rep", 1)
    given, near, far, _ = lax.optimization_barrier((latent, near, far, upper))
    besides = [swap(piece, "tensor", 1) for piece in (given, near, far)]
    choices = [query, second_query, passed]
    *first, query = score_call("score_here", [given, near, far], w_up, choices, pick)
    corner, first[2] = lax.optimization_barrier((corner, first[2]))
    corner += [swap(piece, "tensor", 1) for piece in corner]
    second = list(score_call("score_beside", besides, w_up, query))
    corner[2], second[2] = lax.optimization_barrier((corner[2], second[2]))
    third = score_call("score_corner", corner, w_up, query)
    depth = rows // new_count * head_size
    (attended,) = call(
        lambda *refs: attend_kernel(tokens, *refs),
        "attend",
        [shape((new_count, depth), BF16)],
        [*first, *second, *third],
        16,
        scratch=[pltpu.VMEM((rows, head_size), F32)],
        cost=cost(0, 0),
    )
    attended_other = swap(attended, "seq", 1)
    columns = w_out.shape[1]
    tile = min(512, columns // 2)
    (partial,) = call(
        lambda *refs: project_kernel(tile, *refs),
        "project",
        [shape((2, new_count, columns // 2), F32)],
        [attended, held],
        12,
        cost=cost(0, 0),
    )

    quarter = (new_count, columns // 4)

    def project_more(other, own, kept):
        return call(
            lambda *refs: project_more_kernel(tile, own, kept, *refs),
            "project_own" if own else "project_sent",
            [shape(quarter, F32)],
            [other, held_kept if own else held_sent, partial],
            12,
            cost=cost(0, 0),
        )[0]

    given = swap(project_more(attended_other, False, False), "tensor", 1)
    operands = [project_more(attended_other, True, False), given]
    operands[0], other = lax.optimization_barrier((operands[0], attended_other))
    kept = project_more(other, False, True)
    (given,) = call(add_kernel, "add", [shape(quarter, F32)], operands, 8, cost=cost(0, 0))
    other, given, kept = lax.optimization_barrier((attended_other, given, kept))
    given = swap(given, "tensor", 2)
    kept = swap(kept, "tensor", 1)
    operands = [project_more(other, True, True), kept, given]
    (own,) = call(sum_kernel, "sum", [shape(quarter, BF16)], operands, 8, cost=cost(0, 0))

    def reply(order):
        pairs = [(p * 4 + t, r * 4 + t) for r, p in enumerate(order) for t in range(4)]
        crossed = [(source, target ^ 2) for source, target in pairs]
        axes = ("rep", "tensor")

        def run(value):
            across = lax.ppermute(value, axes, crossed)
            if order == tuple(range(len(order))):
                return value, across
            return lax.ppermute(value, axes, pairs), across

        return run

    own, across = lax.switch(index[0], [reply(order) for order in orders], own)
    beside, last = swap(own, "tensor", 1), swap(across, "tensor", 1)
    joined = join((0, 1), [own, across], None)
    return join((2, 3), [beside, last], joined)


def shards(key_value_rows, queries, w_comp, latent_gain, w_up, w_out, replica_order):
    orders = list(itertools.permutations(range(lax.axis_size("rep"))))
    index = order_index(replica_order, orders)
    query = route(queries[0], index, orders, False)
    rows = key_value_rows[0]
    latent = compress(rows.reshape(rows.shape[0], -1), w_comp, latent_gain)
    latent = lax.all_gather(latent, "tensor", axis=0, tiled=True)
    groups = w_up.shape[0]
    lifted = jnp.einsum("tf,gfy->tgy", latent, w_up, preferred_element_type=F32).astype(BF16)
    head_size = query.shape[-1]
    new_count = query.shape[0]
    keys = lifted[..., :head_size]
    values = lifted[..., head_size:]
    grouped_heads = query.reshape(new_count, groups, -1, head_size)
    scores = jnp.einsum(
        "nghd,tgd->nght", grouped_heads, keys, preferred_element_type=F32
    ) * head_size ** (-0.5)
    top = lax.pmax(jnp.max(scores, axis=-1), "seq")
    expo = jnp.exp(scores - top[..., None])
    total = jnp.sum(expo, axis=-1)
    summed = jnp.einsum("nght,tgd->nghd", expo.astype(BF16), values, preferred_element_type=F32)
    summed, total = lax.psum((summed, total), "seq")
    attended = (summed / total[..., None]).astype(BF16).reshape(new_count, -1)
    attended = route(attended, index, orders, True)
    return lax.psum(dot(attended, w_out), "tensor").astype(BF16)[None]


def solution(mesh):
    placed = (
        P("rep", ("seq", "tensor"), None, None),
        P("rep", None, "tensor", None),
        P(),
        P(),
        P("tensor", None, None),
        P("tensor", "seq"),
        P(),
    )
    square = all(mesh.shape[axis] == size for axis, size in (("seq", 2), ("rep", 4), ("tensor", 4)))
    return jax.shard_map(
        square_shards if square else shards,
        mesh=mesh,
        in_specs=placed,
        out_specs=P("rep", None, "seq"),
        check_vma=False,
    )
```

profile of v0, /device:TPU:0, one launch (start us, length us, event | category | flops | bytes accessed | tf_op | source)
XLA Modules:
  0.0 66.4 jit_solution(9636830399251869753)
XLA Ops:
  0.0 3.8 %compress.1 = (bf16[384,512]{1,0:T(8,128)(2,1)S(1)}, bf16[512,128]{1,0:T(8,128)(2,1)S(1)}, s32[1]{0:T(128)}, s32[2]{0:T(128)S(1)}) custom-call(s32[4]{0:T(128)} %refs_0_.1, bf16[1,384,8,256]{3,2,1,0:T(8,128)(2,1)} %refs_1_.1, bf16[2048,512]{1,0:T(8,128)(2,1)} %refs_2_.1, bf16[512]{0:T(512)(128)(2,1)} %refs_3_.2, bf16[1,64,16,128]{3,2,1,0:T(8,128)(2,1)} %refs_4_.3), custom_call_target="tpu_custom_call" | custom-call | tf_op jit(solution)/shard_map/compress/pallas_call | solution.py:31
  3.8 3.0 %collective-permute-start.48 = (bf16[384,512]{1,0:T(8,128)(2,1)S(1)}, bf16[384,512]{1,0:T(8,128)(2,1)S(1)}, u32[]{:S(2)}, u32[]{:S(2)}) collective-permute-start(bf16[384,512]{1,0:T(8,128)(2,1)S(1)} %get-tuple-element.76.refs_1_), channel_id=1, source_target_pairs={{0,2},{1,3},{2,0},{3,1},{4,6},{5,7},{6,4},{7,5},{8,10},{9,11},{10,... | collective-permute-start | bytes 1179656 | tf_op jit(solution)/shard_map/ppermute | solution.py:81
  6.8 1.5 %collective-permute-start.47 = (bf16[384,512]{1,0:T(8,128)(2,1)S(1)}, bf16[384,512]{1,0:T(8,128)(2,1)S(1)}, u32[]{:S(2)}, u32[]{:S(2)}) collective-permute-start(bf16[384,512]{1,0:T(8,128)(2,1)S(1)} %get-tuple-element.76.refs_1_), channel_id=1, source_target_pairs={{0,16},{16,0},{1,17},{17,1},{2,18},{18,2},{3,19},{19,3},{4,20},{20... | collective-permute-start | bytes 1179656 | tf_op jit(solution)/shard_map/ppermute | solution.py:81
  8.3 2.6 %collective-permute-start.49 = (bf16[512,128]{1,0:T(8,128)(2,1)S(1)}, bf16[512,128]{1,0:T(8,128)(2,1)S(1)}, u32[]{:S(2)}, u32[]{:S(2)}) collective-permute-start(bf16[512,128]{1,0:T(8,128)(2,1)S(1)} %get-tuple-element.70.own_ref.refs_5_), channel_id=1, source_target_pairs={{0,8},{4,12},{8,0},{12,4},{1,9},{5,13},{9,1},{13,5},{2,10},{6,14},... | collective-permute-start | bytes 393224 | tf_op jit(solution)/shard_map/ppermute | solution.py:81
  10.9 6.0 %fetch.1 = (bf16[1024,4096]{1,0:T(8,128)(2,1)S(1)}, bf16[1024,2048]{1,0:T(8,128)(2,1)S(1)}, bf16[1024,2048]{1,0:T(8,128)(2,1)S(1)}) custom-call(bf16[2048,4096]{1,0:T(8,128)(2,1)} %weight_ref.1), custom_call_target="tpu_custom_call" | custom-call | tf_op jit(solution)/shard_map/fetch/pallas_call | solution.py:31
  16.9 0.0 collective-permute-done.49.second_ref.refs_6_
  16.9 0.6 pass.1
  17.4 1.6 %collective-permute-start.50 = (bf16[512,128]{1,0:T(8,128)(2,1)S(1)}, bf16[512,128]{1,0:T(8,128)(2,1)S(1)}, u32[]{:S(2)}, u32[]{:S(2)}) collective-permute-start(bf16[512,128]{1,0:T(8,128)(2,1)S(1)} %pass.1), channel_id=1, source_target_pairs={{0,4},{4,0},{8,12},{12,8},{1,5},{5,1},{9,13},{13,9},{2,6},{6,2},{1... | collective-permute-start | bytes 393224 | tf_op jit(solution)/shard_map/ppermute | solution.py:81
  19.1 0.0 collective-permute-done.48.far_ref.refs_3_
  19.1 0.0 collective-permute-done.47.near_ref.refs_2_
  19.1 0.6 collective-permute-start.51
  19.7 0.5 collective-permute-start.52
  20.2 0.5 collective-permute-start.54
  20.7 1.7 %collective-permute-done.50.refs_7_ = bf16[512,128]{1,0:T(8,128)(2,1)S(1)} collective-permute-done((bf16[512,128]{1,0:T(8,128)(2,1)S(1)}, bf16[512,128]{1,0:T(8,128)(2,1)S(1)}, u32[]{:S(2)}, u32[]{:S(2)}) %collective-permute-start.50) | collective-permute-done | bytes 131104 | tf_op jit(solution)/shard_map/ppermute | solution.py:81
  22.5 0.0 collective-permute-start.55
  22.5 1.6 %score_here.1 = (f32[1152,512]{1,0:T(8,128)S(1)}, bf16[1152,128]{1,0:T(8,128)(2,1)S(1)}, f32[8,512]{1,0:T(8,128)S(1)}, bf16[512,128]{1,0:T(8,128)(2,1)S(1)}) custom-call(s32[2]{0:T(128)S(1)} %get-tuple-element.68.pick_ref.refs_0_, bf16[384,512]{1,0:T(8,128)(2,1)S(1)} %get-tuple-element.76.refs_1_, ...), custom_call_target="tpu_custom_call" | custom-call | tf_op jit(solution)/shard_map/score_here/pallas_call | solution.py:31
  24.1 1.3 %collective-permute-done.52.refs_1_ = bf16[192,512]{1,0:T(8,128)(2,1)S(1)} collective-permute-done((bf16[192,512]{1,0:T(8,128)(2,1)S(1)}, bf16[192,512]{1,0:T(8,128)(2,1)S(1)}, u32[]{:S(2)}, u32[]{:S(2)}) %collective-permute-start.52) | collective-permute-done | bytes 196640 | tf_op jit(solution)/shard_map/ppermute | solution.py:81
  25.4 0.0 collective-permute-done.51.refs_0_
  25.4 0.0 collective-permute-start.56
  25.4 0.5 collective-permute-start.57
  25.9 0.0 collective-permute-done.54.refs_1_
  25.9 0.0 collective-permute-done.55.refs_2_
  25.9 1.0 %score_beside.1 = (f32[1152,512]{1,0:T(8,128)S(1)}, bf16[1152,128]{1,0:T(8,128)(2,1)S(1)}, f32[8,512]{1,0:T(8,128)S(1)}) custom-call(bf16[384,512]{1,0:T(8,128)(2,1)S(1)} %collective-permute-done.53.refs_0_, bf16[384,512]{1,0:T(8,128)(2,1)S(1)} %collective-permute-done.54.refs_1_, bf16[384,512]{1,0:T(8,128)(2,1)S(1)} %collective-permute-done.55.refs_2_, ...), custom_call_target="tpu_custom_call" | custom-call | tf_op jit(solution)/shard_map/score_beside/pallas_call | solution.py:31
  26.9 0.0 collective-permute-done.56.refs_2_
  26.9 0.2 collective-permute-done.57.refs_3_
  27.1 0.7 %score_corner.1 = (f32[768,512]{1,0:T(8,128)S(1)}, bf16[768,128]{1,0:T(8,128)(2,1)S(1)}, f32[8,512]{1,0:T(8,128)S(1)}) custom-call(bf16[192,512]{1,0:T(8,128)(2,1)S(1)} %collective-permute-done.51.refs_0_, bf16[192,512]{1,0:T(8,128)(2,1)S(1)} %collective-permute-done.52.refs_1_, bf16[192,512]{1,0:T(8,128)(2,1)S(1)} %collective-permute-done.56.refs_2_, ...), custom_call_target="tpu_custom_call" | custom-call | tf_op jit(solution)/shard_map/score_corner/pallas_call | solution.py:31
  27.9 1.4 %attend.1.refs_0_ = bf16[64,1024]{1,0:T(8,128)(2,1)S(1)} custom-call(f32[1152,512]{1,0:T(8,128)S(1)} %get-tuple-element.79.refs_0_, bf16[1152,128]{1,0:T(8,128)(2,1)S(1)} %get-tuple-element.80.refs_1_, f32[8,512]{1,0:T(8,128)S(1)} %get-tuple-element.83.refs_2_, f32[1152,512]{1,0:T(8,128)S(1)} %get-tuple-element.85.refs_3_, ...), custom_call_target="tpu_custom_call" | custom-call | tf_op jit(solution)/shard_map/attend/pallas_call | solution.py:31
  29.3 0.6 collective-permute-start.58
  29.9 1.5 %project.1.refs_2_ = f32[2,64,2048]{2,1,0:T(8,128)S(1)} custom-call(bf16[64,1024]{1,0:T(8,128)(2,1)S(1)} %attend.1.refs_0_, bf16[1024,4096]{1,0:T(8,128)(2,1)S(1)} %get-tuple-element.96.refs_1_), custom_call_target="tpu_custom_call" | custom-call | tf_op jit(solution)/shard_map/project/pallas_call | solution.py:31
  31.4 3.6 %collective-permute-done.58.refs_0_ = bf16[64,1024]{1,0:T(8,128)(2,1)S(1)} collective-permute-done((bf16[64,1024]{1,0:T(8,128)(2,1)S(1)}, bf16[64,1024]{1,0:T(8,128)(2,1)S(1)}, u32[]{:S(2)}, u32[]{:S(2)}) %collective-permute-start.58) | collective-permute-done | bytes 131104 | tf_op jit(solution)/shard_map/ppermute | solution.py:81
  35.0 0.5 project_sent.2
  35.5 0.1 collective-permute-start.59
  35.6 0.5 project_own.2.one_ref
  36.1 0.5 project_sent.3
  36.6 0.5 collective-permute-done.59.other_ref
  37.1 0.2 collective-permute-start.60
  37.3 1.5 %collective-permute-start.61 = (f32[64,1024]{1,0:T(8,128)S(1)}, f32[64,1024]{1,0:T(8,128)S(1)}, u32[]{:S(2)}, u32[]{:S(2)}) collective-permute-start(f32[64,1024]{1,0:T(8,128)S(1)} %add.1), channel_id=1, source_target_pairs={{0,2},{1,3},{2,0},{3,1},{4,6},{5,7},{6,4},{7,5},{8,10},{9,11},{10,... | collective-permute-start | bytes 786440 | tf_op jit(solution)/shard_map/ppermute | solution.py:81
  39.5 0.5 project_own.3.own_ref
  40.0 5.9 %collective-permute-done.61.across_ref = f32[64,1024]{1,0:T(8,128)S(1)} collective-permute-done((f32[64,1024]{1,0:T(8,128)S(1)}, f32[64,1024]{1,0:T(8,128)S(1)}, u32[]{:S(2)}, u32[]{:S(2)}) %collective-permute-start.61) | collective-permute-done | bytes 262176 | tf_op jit(solution)/shard_map/ppermute | solution.py:81
  45.9 17.5 %conditional.1 = (bf16[64,1024]{1,0:T(8,128)(2,1)}, bf16[64,1024]{1,0:T(8,128)(2,1)}) conditional(s32[]{:T(128)} %bitcast, bf16[64,1024]{1,0:T(8,128)(2,1)S(1)} %sum.1, bf16[64,1024]{1,0:T(8,128)(2,1)S(1)} %sum.1, bf16[64,1024]{1,0:T(8,128)(2,1)S(1)} %sum.1, bf16[64,1024]{1,0:T(8,128)(2,1)S(1)} %sum.1, ...), branch_computations={%region_0.0_spmd, %region_1.0_spmd, %region_2.0_spmd, %region_3.0_... | conditional | bytes 1048672 | solution.py:454
  46.0 3.9 %collective-permute-start.46 = (bf16[64,1024]{1,0:T(8,128)(2,1)S(1)}, bf16[64,1024]{1,0:T(8,128)(2,1)}, u32[]{:S(2)}, u32[]{:S(2)}) collective-permute-start(bf16[64,1024]{1,0:T(8,128)(2,1)S(1)} %param.23), channel_id=1, source_target_pairs={{12,2},{13,3},{14,0},{15,1},{8,6},{9,7},{10,4},{11,5},{4,10},{5,11... | collective-permute-start | bytes 393224 | tf_op jit(solution)/shard_map/cond/branch_23_fun/ppermute | solution.py:447
  50.0 5.7 %collective-permute-start.45 = (bf16[64,1024]{1,0:T(8,128)(2,1)S(1)}, bf16[64,1024]{1,0:T(8,128)(2,1)}, u32[]{:S(2)}, u32[]{:S(2)}) collective-permute-start(bf16[64,1024]{1,0:T(8,128)(2,1)S(1)} %param.23), channel_id=1, source_target_pairs={{12,0},{13,1},{14,2},{15,3},{8,4},{9,5},{10,6},{11,7},{4,8},{5,9},... | collective-permute-start | bytes 393224 | tf_op jit(solution)/shard_map/cond/branch_23_fun/ppermute | solution.py:450
  55.7 2.9 %collective-permute-done.46 = bf16[64,1024]{1,0:T(8,128)(2,1)} collective-permute-done((bf16[64,1024]{1,0:T(8,128)(2,1)S(1)}, bf16[64,1024]{1,0:T(8,128)(2,1)}, u32[]{:S(2)}, u32[]{:S(2)}) %collective-permute-start.46) | collective-permute-done | bytes 131104 | tf_op jit(solution)/shard_map/cond/branch_23_fun/ppermute | solution.py:447
  58.6 4.8 %collective-permute-done.45 = bf16[64,1024]{1,0:T(8,128)(2,1)} collective-permute-done((bf16[64,1024]{1,0:T(8,128)(2,1)S(1)}, bf16[64,1024]{1,0:T(8,128)(2,1)}, u32[]{:S(2)}, u32[]{:S(2)}) %collective-permute-start.45) | collective-permute-done | bytes 131104 | tf_op jit(solution)/shard_map/cond/branch_23_fun/ppermute | solution.py:450
  63.4 0.5 collective-permute-start.63
  64.0 1.7 %join.2.refs_2_ = bf16[1,64,4096]{2,1,0:T(8,128)(2,1)} custom-call(bf16[64,1024]{1,0:T(8,128)(2,1)} %get-tuple-element.103.refs_0_, bf16[64,1024]{1,0:T(8,128)(2,1)} %get-tuple-element.104.refs_1_), custom_call_target="tpu_custom_call" | custom-call | tf_op jit(solution)/shard_map/join/pallas_call | solution.py:321
  65.7 0.0 collective-permute-done.63.refs_1_
  65.7 0.7 %join.3 = bf16[1,64,4096]{2,1,0:T(8,128)(2,1)} custom-call(bf16[64,1024]{1,0:T(8,128)(2,1)S(1)} %collective-permute-done.62.refs_0_, bf16[64,1024]{1,0:T(8,128)(2,1)S(1)} %collective-permute-done.63.refs_1_, bf16[1,64,4096]{2,1,0:T(8,128)(2,1)} %join.2.refs_2_), custom_call_target="tpu_custom_call", output_to_operand_aliasing={{}: (2, {})} | custom-call | tf_op jit(solution)/shard_map/join/pallas_call | solution.py:321
  (10 shorter events, 0.1 us)
Async XLA Ops:
  3.8 15.3 %collective-permute-start.48 = (bf16[384,512]{1,0:T(8,128)(2,1)S(1)}, bf16[384,512]{1,0:T(8,128)(2,1)S(1)}, u32[]{:S(2)}, u32[]{:S(2)}) collective-permute-start(bf16[384,512]{1,0:T(8,128)(2,1)S(1)} %get-tuple-element.76.refs_1_), channel_id=1, source_target_pairs={{0,2},{1,3},{2,0},{3,1},{4,6},{5,7},{6,4},{7,5},{8,10},{9,11},{10,... | collective-permute-start | bytes 1179656 | tf_op jit(solution)/shard_map/ppermute | solution.py:81
  6.8 12.3 %collective-permute-start.47 = (bf16[384,512]{1,0:T(8,128)(2,1)S(1)}, bf16[384,512]{1,0:T(8,128)(2,1)S(1)}, u32[]{:S(2)}, u32[]{:S(2)}) collective-permute-start(bf16[384,512]{1,0:T(8,128)(2,1)S(1)} %get-tuple-element.76.refs_1_), channel_id=1, source_target_pairs={{0,16},{16,0},{1,17},{17,1},{2,18},{18,2},{3,19},{19,3},{4,20},{20... | collective-permute-start | bytes 1179656 | tf_op jit(solution)/shard_map/ppermute | solution.py:81
  8.3 14.2 %copy-start = (bf16[2,512,256]{2,1,0:T(8,128)(2,1)S(1)}, bf16[2,512,256]{2,1,0:T(8,128)(2,1)}, u32[]{:S(2)}) copy-start(bf16[2,512,256]{2,1,0:T(8,128)(2,1)} %refs_4_.5) | copy-start | bytes 1572868
  8.3 8.6 %collective-permute-start.49 = (bf16[512,128]{1,0:T(8,128)(2,1)S(1)}, bf16[512,128]{1,0:T(8,128)(2,1)S(1)}, u32[]{:S(2)}, u32[]{:S(2)}) collective-permute-start(bf16[512,128]{1,0:T(8,128)(2,1)S(1)} %get-tuple-element.70.own_ref.refs_5_), channel_id=1, source_target_pairs={{0,8},{4,12},{8,0},{12,4},{1,9},{5,13},{9,1},{13,5},{2,10},{6,14},... | collective-permute-start | bytes 393224 | tf_op jit(solution)/shard_map/ppermute | solution.py:81
  17.4 5.0 %collective-permute-start.50 = (bf16[512,128]{1,0:T(8,128)(2,1)S(1)}, bf16[512,128]{1,0:T(8,128)(2,1)S(1)}, u32[]{:S(2)}, u32[]{:S(2)}) collective-permute-start(bf16[512,128]{1,0:T(8,128)(2,1)S(1)} %pass.1), channel_id=1, source_target_pairs={{0,4},{4,0},{8,12},{12,8},{1,5},{5,1},{9,13},{13,9},{2,6},{6,2},{1... | collective-permute-start | bytes 393224 | tf_op jit(solution)/shard_map/ppermute | solution.py:81
  19.1 6.3 %collective-permute-start.51 = (bf16[192,512]{1,0:T(8,128)(2,1)S(1)}, bf16[192,512]{1,0:T(8,128)(2,1)S(1)}, u32[]{:S(2)}, u32[]{:S(2)}) collective-permute-start(bf16[192,512]{1,0:T(8,128)(2,1)S(1)} %get-tuple-element.75), channel_id=1, source_target_pairs={{0,2},{1,3},{2,0},{3,1},{4,6},{5,7},{6,4},{7,5},{8,10},{9,11},{10,... | collective-permute-start | bytes 589832 | tf_op jit(solution)/shard_map/ppermute | solution.py:81
  19.7 5.7 %collective-permute-start.52 = (bf16[192,512]{1,0:T(8,128)(2,1)S(1)}, bf16[192,512]{1,0:T(8,128)(2,1)S(1)}, u32[]{:S(2)}, u32[]{:S(2)}) collective-permute-start(bf16[192,512]{1,0:T(8,128)(2,1)S(1)} %get-tuple-element.81), channel_id=1, source_target_pairs={{0,16},{16,0},{1,17},{17,1},{2,18},{18,2},{3,19},{19,3},{4,20},{20... | collective-permute-start | bytes 589832 | tf_op jit(solution)/shard_map/ppermute | solution.py:81
  20.2 5.7 %collective-permute-start.53 = (bf16[384,512]{1,0:T(8,128)(2,1)S(1)}, bf16[384,512]{1,0:T(8,128)(2,1)S(1)}, u32[]{:S(2)}, u32[]{:S(2)}) collective-permute-start(bf16[384,512]{1,0:T(8,128)(2,1)S(1)} %get-tuple-element.76.refs_1_), channel_id=1, source_target_pairs={{0,1},{1,0},{2,3},{3,2},{4,5},{5,4},{6,7},{7,6},{8,9},{9,8},{10,11... | collective-permute-start | bytes 1179656 | tf_op jit(solution)/shard_map/ppermute | solution.py:81
  20.2 5.7 %collective-permute-start.54 = (bf16[384,512]{1,0:T(8,128)(2,1)S(1)}, bf16[384,512]{1,0:T(8,128)(2,1)S(1)}, u32[]{:S(2)}, u32[]{:S(2)}) collective-permute-start(bf16[384,512]{1,0:T(8,128)(2,1)S(1)} %collective-permute-done.47.near_ref.refs_2_), channel_id=1, source_target_pairs={{0,1},{1,0},{2,3},{3,2},{4,5},{5,4},{6,7},{7,6},{8,9},{9,8},{10,11... | collective-permute-start | bytes 1179656 | tf_op jit(solution)/shard_map/ppermute | solution.py:81
  22.5 3.4 %collective-permute-start.55 = (bf16[384,512]{1,0:T(8,128)(2,1)S(1)}, bf16[384,512]{1,0:T(8,128)(2,1)S(1)}, u32[]{:S(2)}, u32[]{:S(2)}) collective-permute-start(bf16[384,512]{1,0:T(8,128)(2,1)S(1)} %collective-permute-done.48.far_ref.refs_3_), channel_id=1, source_target_pairs={{0,1},{1,0},{2,3},{3,2},{4,5},{5,4},{6,7},{7,6},{8,9},{9,8},{10,11... | collective-permute-start | bytes 1179656 | tf_op jit(solution)/shard_map/ppermute | solution.py:81
  25.4 1.5 %collective-permute-start.56 = (bf16[192,512]{1,0:T(8,128)(2,1)S(1)}, bf16[192,512]{1,0:T(8,128)(2,1)S(1)}, u32[]{:S(2)}, u32[]{:S(2)}) collective-permute-start(bf16[192,512]{1,0:T(8,128)(2,1)S(1)} %collective-permute-done.51.refs_0_), channel_id=1, source_target_pairs={{0,1},{1,0},{2,3},{3,2},{4,5},{5,4},{6,7},{7,6},{8,9},{9,8},{10,11... | collective-permute-start | bytes 589832 | tf_op jit(solution)/shard_map/ppermute | solution.py:81
  25.4 1.7 %collective-permute-start.57 = (bf16[192,512]{1,0:T(8,128)(2,1)S(1)}, bf16[192,512]{1,0:T(8,128)(2,1)S(1)}, u32[]{:S(2)}, u32[]{:S(2)}) collective-permute-start(bf16[192,512]{1,0:T(8,128)(2,1)S(1)} %collective-permute-done.52.refs_1_), channel_id=1, source_target_pairs={{0,1},{1,0},{2,3},{3,2},{4,5},{5,4},{6,7},{7,6},{8,9},{9,8},{10,11... | collective-permute-start | bytes 589832 | tf_op jit(solution)/shard_map/ppermute | solution.py:81
  29.3 5.7 %collective-permute-start.58 = (bf16[64,1024]{1,0:T(8,128)(2,1)S(1)}, bf16[64,1024]{1,0:T(8,128)(2,1)S(1)}, u32[]{:S(2)}, u32[]{:S(2)}) collective-permute-start(bf16[64,1024]{1,0:T(8,128)(2,1)S(1)} %attend.1.refs_0_), channel_id=1, source_target_pairs={{0,16},{16,0},{1,17},{17,1},{2,18},{18,2},{3,19},{19,3},{4,20},{20... | collective-permute-start | bytes 393224 | tf_op jit(solution)/shard_map/ppermute | solution.py:81
  35.5 1.6 %collective-permute-start.59 = (f32[64,1024]{1,0:T(8,128)S(1)}, f32[64,1024]{1,0:T(8,128)S(1)}, u32[]{:S(2)}, u32[]{:S(2)}) collective-permute-start(f32[64,1024]{1,0:T(8,128)S(1)} %project_sent.2), channel_id=1, source_target_pairs={{0,1},{1,0},{2,3},{3,2},{4,5},{5,4},{6,7},{7,6},{8,9},{9,8},{10,11... | collective-permute-start | bytes 786440 | tf_op jit(solution)/shard_map/ppermute | solution.py:81
  37.1 2.9 %collective-permute-start.60 = (f32[64,1024]{1,0:T(8,128)S(1)}, f32[64,1024]{1,0:T(8,128)S(1)}, u32[]{:S(2)}, u32[]{:S(2)}) collective-permute-start(f32[64,1024]{1,0:T(8,128)S(1)} %project_sent.3), channel_id=1, source_target_pairs={{0,1},{1,0},{2,3},{3,2},{4,5},{5,4},{6,7},{7,6},{8,9},{9,8},{10,11... | collective-permute-start | bytes 786440 | tf_op jit(solution)/shard_map/ppermute | solution.py:81
  37.3 8.6 %collective-permute-start.61 = (f32[64,1024]{1,0:T(8,128)S(1)}, f32[64,1024]{1,0:T(8,128)S(1)}, u32[]{:S(2)}, u32[]{:S(2)}) collective-permute-start(f32[64,1024]{1,0:T(8,128)S(1)} %add.1), channel_id=1, source_target_pairs={{0,2},{1,3},{2,0},{3,1},{4,6},{5,7},{6,4},{7,5},{8,10},{9,11},{10,... | collective-permute-start | bytes 786440 | tf_op jit(solution)/shard_map/ppermute | solution.py:81
  46.0 12.6 %collective-permute-start.46 = (bf16[64,1024]{1,0:T(8,128)(2,1)S(1)}, bf16[64,1024]{1,0:T(8,128)(2,1)}, u32[]{:S(2)}, u32[]{:S(2)}) collective-permute-start(bf16[64,1024]{1,0:T(8,128)(2,1)S(1)} %param.23), channel_id=1, source_target_pairs={{12,2},{13,3},{14,0},{15,1},{8,6},{9,7},{10,4},{11,5},{4,10},{5,11... | collective-permute-start | bytes 393224 | tf_op jit(solution)/shard_map/cond/branch_23_fun/ppermute | solution.py:447
  50.0 13.5 %collective-permute-start.45 = (bf16[64,1024]{1,0:T(8,128)(2,1)S(1)}, bf16[64,1024]{1,0:T(8,128)(2,1)}, u32[]{:S(2)}, u32[]{:S(2)}) collective-permute-start(bf16[64,1024]{1,0:T(8,128)(2,1)S(1)} %param.23), channel_id=1, source_target_pairs={{12,0},{13,1},{14,2},{15,3},{8,4},{9,5},{10,6},{11,7},{4,8},{5,9},... | collective-permute-start | bytes 393224 | tf_op jit(solution)/shard_map/cond/branch_23_fun/ppermute | solution.py:450
  63.4 2.2 %collective-permute-start.62 = (bf16[64,1024]{1,0:T(8,128)(2,1)}, bf16[64,1024]{1,0:T(8,128)(2,1)S(1)}, u32[]{:S(2)}, u32[]{:S(2)}) collective-permute-start(bf16[64,1024]{1,0:T(8,128)(2,1)} %get-tuple-element.103.refs_0_), channel_id=1, source_target_pairs={{0,1},{1,0},{2,3},{3,2},{4,5},{5,4},{6,7},{7,6},{8,9},{9,8},{10,11... | collective-permute-start | bytes 393224 | tf_op jit(solution)/shard_map/ppermute | solution.py:81
  63.4 2.2 %collective-permute-start.63 = (bf16[64,1024]{1,0:T(8,128)(2,1)}, bf16[64,1024]{1,0:T(8,128)(2,1)S(1)}, u32[]{:S(2)}, u32[]{:S(2)}) collective-permute-start(bf16[64,1024]{1,0:T(8,128)(2,1)} %get-tuple-element.104.refs_1_), channel_id=1, source_target_pairs={{0,1},{1,0},{2,3},{3,2},{4,5},{5,4},{6,7},{7,6},{8,9},{9,8},{10,11... | collective-permute-start | bytes 393224 | tf_op jit(solution)/shard_map/ppermute | solution.py:81
where the time goes:
time: 67.4 us; the launch traced here: 66.4 us
  starting transfers between devices  23.4 us (35%)
  Pallas kernels  21 us (31%)
  waiting for transfers between devices  21 us (31%)
  between operations  0.83 us (1%)
    pallas_call x15, Pallas kernels, call(): pl.pallas_call(body, out_shape=outs, in_specs=specs, out_specs=out_specs,...  18.6 us
    ppermute x17, starting transfers between devices, swap(): return lax.ppermute(value, axis, pairs)  13.7 us
    ppermute x17, waiting for transfers between devices, swap(): return lax.ppermute(value, axis, pairs)  13.3 us
    ppermute x1, starting transfers between devices, run(): return (lax.ppermute(value, axes, pairs), across)  5.72 us
    ppermute x1, waiting for transfers between devices, run(): return (lax.ppermute(value, axes, pairs), across)  4.82 us
    ppermute x1, starting transfers between devices, run(): across = lax.ppermute(value, axes, crossed)  3.94 us
    ppermute x1, waiting for transfers between devices, run(): across = lax.ppermute(value, axes, crossed)  2.95 us
    pallas_call x2, Pallas kernels, join(): pl.pallas_call(lambda *refs: join_kernel(places, *refs), out_shape=shape(...  2.42 us
  transfers between devices with their start and end apart: 19, of which 8 were waited for; matrix products, arithmetic and copies ran while one was open for 0% of the time, Pallas kernels for 21%

commit v1 on v0

--- a/solution.py
+++ b/solution.py
@@ -260,8 +260,9 @@
             summed += lax.dot_general(
                 value_ref[at], expo.astype(BF16), (((0,), (0,)), ((), ())), preferred_element_type=F32
             )
-    turned[...] = (summed / total).T
-    heads = turned.shape[0] // new_count
+    rows = top.shape[1]
+    turned[:rows] = (summed / total).T
+    heads = rows // new_count
     for head in range(heads):
         out_ref[:, head * head_size : (head + 1) * head_size] = turned[
             pl.ds(head, new_count, stride=heads), :
@@ -350,7 +351,7 @@
             pltpu.VMEM(w_comp.shape, BF16),
             pltpu.VMEM(latent_gain.shape, BF16),
             pltpu.VMEM(queries.shape[1:], BF16),
-            pltpu.VMEM((width // 128, tokens * all_groups, 128), F32),
+            pltpu.VMEM((width // 128, (tokens + 1) * all_groups, 128), F32),
             pltpu.VMEM((tokens, all_groups * width), BF16),
             pltpu.SemaphoreType.DMA((3 + chunks + all_groups,)),
         ],
@@ -400,7 +401,7 @@
         [shape((new_count, depth), BF16)],
         [*first, *second, *third],
         16,
-        scratch=[pltpu.VMEM((rows, head_size), F32)],
+        scratch=[pltpu.VMEM((rows + rows // new_count, head_size), F32)],
         cost=cost(0, 0),
     )
     attended_other = swap(attended, "seq", 1)
@@ -444,6 +445,9 @@
         axes = ("rep", "tensor")
 
         def run(value):
+            if max(abs(p - r) for r, p in enumerate(order)) > 2:
+                own = lax.ppermute(value, axes, pairs)
+                return own, swap(own, "tensor", 2)
             across = lax.ppermute(value, axes, crossed)
             if order == tuple(range(len(order))):
                 return value, across

time: 67.4 us -> 57.9 us (0.86)
  the two profiles are of different devices: /device:TPU:0 before, /device:TPU:9 now
where the time goes in v1:
time: 57.9 us; the launch traced here: 58.2 us
  starting transfers between devices  22.4 us (39%)
  Pallas kernels  21 us (36%)
  waiting for transfers between devices  13.8 us (24%)
  between operations  0.84 us (1%)
    pallas_call x15, Pallas kernels, call(): pl.pallas_call(body, out_shape=outs, in_specs=specs, out_specs=out_specs,...  18.6 us
    ppermute x17, starting transfers between devices, swap(): return lax.ppermute(value, axis, pairs)  17.2 us
    ppermute x17, waiting for transfers between devices, swap(): return lax.ppermute(value, axis, pairs)  9.04 us
    ppermute x1, waiting for transfers between devices, run(): return (lax.ppermute(value, axes, pairs), across)  4.28 us
    ppermute x1, starting transfers between devices, run(): across = lax.ppermute(value, axes, crossed)  3.35 us
    pallas_call x2, Pallas kernels, join(): pl.pallas_call(lambda *refs: join_kernel(places, *refs), out_shape=shape(...  2.42 us
    ppermute x1, starting transfers between devices, run(): return (lax.ppermute(value, axes, pairs), across)  1.93 us
  transfers between devices with their start and end apart: 19, of which 7 were waited for; matrix products, arithmetic and copies ran while one was open for 0% of the time, Pallas kernels for 24%

profile of v1, /device:TPU:9, one launch (start us, length us, event | category | flops | bytes accessed | tf_op | source)
XLA Modules:
  0.0 58.2 jit_solution(13094277651242688060)
XLA Ops:
  0.0 3.8 %compress.1 = (bf16[384,512]{1,0:T(8,128)(2,1)S(1)}, bf16[512,128]{1,0:T(8,128)(2,1)S(1)}, s32[1]{0:T(128)}, s32[2]{0:T(128)S(1)}) custom-call(s32[4]{0:T(128)} %refs_0_.1, bf16[1,384,8,256]{3,2,1,0:T(8,128)(2,1)} %refs_1_.1, bf16[2048,512]{1,0:T(8,128)(2,1)} %refs_2_.1, bf16[512]{0:T(512)(128)(2,1)} %refs_3_.2, bf16[1,64,16,128]{3,2,1,0:T(8,128)(2,1)} %refs_4_.3), custom_call_target="tpu_custom_call" | custom-call | tf_op jit(solution)/shard_map/compress/pallas_call | solution.py:31
  3.8 1.3 %collective-permute-start.48 = (bf16[384,512]{1,0:T(8,128)(2,1)S(1)}, bf16[384,512]{1,0:T(8,128)(2,1)S(1)}, u32[]{:S(2)}, u32[]{:S(2)}) collective-permute-start(bf16[384,512]{1,0:T(8,128)(2,1)S(1)} %get-tuple-element.76.refs_1_), channel_id=1, source_target_pairs={{0,2},{1,3},{2,0},{3,1},{4,6},{5,7},{6,4},{7,5},{8,10},{9,11},{10,... | collective-permute-start | bytes 1179656 | tf_op jit(solution)/shard_map/ppermute | solution.py:81
  5.1 1.2 %collective-permute-start.47 = (bf16[384,512]{1,0:T(8,128)(2,1)S(1)}, bf16[384,512]{1,0:T(8,128)(2,1)S(1)}, u32[]{:S(2)}, u32[]{:S(2)}) collective-permute-start(bf16[384,512]{1,0:T(8,128)(2,1)S(1)} %get-tuple-element.76.refs_1_), channel_id=1, source_target_pairs={{0,16},{16,0},{1,17},{17,1},{2,18},{18,2},{3,19},{19,3},{4,20},{20... | collective-permute-start | bytes 1179656 | tf_op jit(solution)/shard_map/ppermute | solution.py:81
  6.3 2.3 %collective-permute-start.49 = (bf16[512,128]{1,0:T(8,128)(2,1)S(1)}, bf16[512,128]{1,0:T(8,128)(2,1)S(1)}, u32[]{:S(2)}, u32[]{:S(2)}) collective-permute-start(bf16[512,128]{1,0:T(8,128)(2,1)S(1)} %get-tuple-element.70.own_ref.refs_5_), channel_id=1, source_target_pairs={{0,8},{4,12},{8,0},{12,4},{1,9},{5,13},{9,1},{13,5},{2,10},{6,14},... | collective-permute-start | bytes 393224 | tf_op jit(solution)/shard_map/ppermute | solution.py:81
  8.6 6.0 %fetch.1 = (bf16[1024,4096]{1,0:T(8,128)(2,1)S(1)}, bf16[1024,2048]{1,0:T(8,128)(2,1)S(1)}, bf16[1024,2048]{1,0:T(8,128)(2,1)S(1)}) custom-call(bf16[2048,4096]{1,0:T(8,128)(2,1)} %weight_ref.1), custom_call_target="tpu_custom_call" | custom-call | tf_op jit(solution)/shard_map/fetch/pallas_call | solution.py:31
  14.6 0.6 pass.1
  15.2 0.2 collective-permute-start.50
  15.4 0.0 collective-permute-done.48.far_ref.refs_3_
  15.4 0.0 collective-permute-done.47.near_ref.refs_2_
  15.4 0.3 collective-permute-start.51
  15.7 0.6 %collective-permute-start.52 = (bf16[192,512]{1,0:T(8,128)(2,1)S(1)}, bf16[192,512]{1,0:T(8,128)(2,1)S(1)}, u32[]{:S(2)}, u32[]{:S(2)}) collective-permute-start(bf16[192,512]{1,0:T(8,128)(2,1)S(1)} %get-tuple-element.81), channel_id=1, source_target_pairs={{0,16},{16,0},{1,17},{17,1},{2,18},{18,2},{3,19},{19,3},{4,20},{20... | collective-permute-start | bytes 589832 | tf_op jit(solution)/shard_map/ppermute | solution.py:81
  16.4 2.4 %collective-permute-start.53 = (bf16[384,512]{1,0:T(8,128)(2,1)S(1)}, bf16[384,512]{1,0:T(8,128)(2,1)S(1)}, u32[]{:S(2)}, u32[]{:S(2)}) collective-permute-start(bf16[384,512]{1,0:T(8,128)(2,1)S(1)} %get-tuple-element.76.refs_1_), channel_id=1, source_target_pairs={{0,1},{1,0},{2,3},{3,2},{4,5},{5,4},{6,7},{7,6},{8,9},{9,8},{10,11... | collective-permute-start | bytes 1179656 | tf_op jit(solution)/shard_map/ppermute | solution.py:81
  18.7 0.0 collective-permute-start.54
  18.7 0.3 collective-permute-done.50.refs_7_
  19.0 2.7 %collective-permute-start.55 = (bf16[384,512]{1,0:T(8,128)(2,1)S(1)}, bf16[384,512]{1,0:T(8,128)(2,1)S(1)}, u32[]{:S(2)}, u32[]{:S(2)}) collective-permute-start(bf16[384,512]{1,0:T(8,128)(2,1)S(1)} %collective-permute-done.48.far_ref.refs_3_), channel_id=1, source_target_pairs={{0,1},{1,0},{2,3},{3,2},{4,5},{5,4},{6,7},{7,6},{8,9},{9,8},{10,11... | collective-permute-start | bytes 1179656 | tf_op jit(solution)/shard_map/ppermute | solution.py:81
  21.7 1.6 %score_here.1 = (f32[1152,512]{1,0:T(8,128)S(1)}, bf16[1152,128]{1,0:T(8,128)(2,1)S(1)}, f32[8,512]{1,0:T(8,128)S(1)}, bf16[512,128]{1,0:T(8,128)(2,1)S(1)}) custom-call(s32[2]{0:T(128)S(1)} %get-tuple-element.68.pick_ref.refs_0_, bf16[384,512]{1,0:T(8,128)(2,1)S(1)} %get-tuple-element.76.refs_1_, ...), custom_call_target="tpu_custom_call" | custom-call | tf_op jit(solution)/shard_map/score_here/pallas_call | solution.py:31
  23.3 0.0 collective-permute-done.51.refs_0_
  23.3 0.2 collective-permute-start.56
  23.5 0.4 collective-permute-start.57
  23.9 0.0 collective-permute-done.53.refs_0_
  23.9 0.0 collective-permute-done.54.refs_1_
  23.9 0.0 collective-permute-done.55.refs_2_
  23.9 1.0 %score_beside.1 = (f32[1152,512]{1,0:T(8,128)S(1)}, bf16[1152,128]{1,0:T(8,128)(2,1)S(1)}, f32[8,512]{1,0:T(8,128)S(1)}) custom-call(bf16[384,512]{1,0:T(8,128)(2,1)S(1)} %collective-permute-done.53.refs_0_, bf16[384,512]{1,0:T(8,128)(2,1)S(1)} %collective-permute-done.54.refs_1_, bf16[384,512]{1,0:T(8,128)(2,1)S(1)} %collective-permute-done.55.refs_2_, ...), custom_call_target="tpu_custom_call" | custom-call | tf_op jit(solution)/shard_map/score_beside/pallas_call | solution.py:31
  24.9 0.0 collective-permute-done.56.refs_2_
  24.9 0.2 collective-permute-done.57.refs_3_
  25.1 0.7 %score_corner.1 = (f32[768,512]{1,0:T(8,128)S(1)}, bf16[768,128]{1,0:T(8,128)(2,1)S(1)}, f32[8,512]{1,0:T(8,128)S(1)}) custom-call(bf16[192,512]{1,0:T(8,128)(2,1)S(1)} %collective-permute-done.51.refs_0_, bf16[192,512]{1,0:T(8,128)(2,1)S(1)} %collective-permute-done.52.refs_1_, bf16[192,512]{1,0:T(8,128)(2,1)S(1)} %collective-permute-done.56.refs_2_, ...), custom_call_target="tpu_custom_call" | custom-call | tf_op jit(solution)/shard_map/score_corner/pallas_call | solution.py:31
  25.8 1.4 %attend.1.refs_0_ = bf16[64,1024]{1,0:T(8,128)(2,1)S(1)} custom-call(f32[1152,512]{1,0:T(8,128)S(1)} %get-tuple-element.79.refs_0_, bf16[1152,128]{1,0:T(8,128)(2,1)S(1)} %get-tuple-element.80.refs_1_, f32[8,512]{1,0:T(8,128)S(1)} %get-tuple-element.83.refs_2_, f32[1152,512]{1,0:T(8,128)S(1)} %get-tuple-element.85.refs_3_, ...), custom_call_target="tpu_custom_call" | custom-call | tf_op jit(solution)/shard_map/attend/pallas_call | solution.py:31
  27.3 0.5 collective-permute-start.58
  27.8 1.6 %project.1.refs_2_ = f32[2,64,2048]{2,1,0:T(8,128)S(1)} custom-call(bf16[64,1024]{1,0:T(8,128)(2,1)S(1)} %attend.1.refs_0_, bf16[1024,4096]{1,0:T(8,128)(2,1)S(1)} %get-tuple-element.96.refs_1_), custom_call_target="tpu_custom_call" | custom-call | tf_op jit(solution)/shard_map/project/pallas_call | solution.py:31
  29.4 2.8 %collective-permute-done.58.refs_0_ = bf16[64,1024]{1,0:T(8,128)(2,1)S(1)} collective-permute-done((bf16[64,1024]{1,0:T(8,128)(2,1)S(1)}, bf16[64,1024]{1,0:T(8,128)(2,1)S(1)}, u32[]{:S(2)}, u32[]{:S(2)}) %collective-permute-start.58) | collective-permute-done | bytes 131104 | tf_op jit(solution)/shard_map/ppermute | solution.py:81
  32.2 0.5 project_sent.2
  32.7 1.1 %collective-permute-start.59 = (f32[64,1024]{1,0:T(8,128)S(1)}, f32[64,1024]{1,0:T(8,128)S(1)}, u32[]{:S(2)}, u32[]{:S(2)}) collective-permute-start(f32[64,1024]{1,0:T(8,128)S(1)} %project_sent.2), channel_id=1, source_target_pairs={{0,1},{1,0},{2,3},{3,2},{4,5},{5,4},{6,7},{7,6},{8,9},{9,8},{10,11... | collective-permute-start | bytes 786440 | tf_op jit(solution)/shard_map/ppermute | solution.py:81
  33.8 0.5 project_own.2.one_ref
  34.3 0.5 project_sent.3
  34.8 0.2 collective-permute-done.59.other_ref
  35.0 0.4 collective-permute-start.60
  35.4 1.1 %collective-permute-start.61 = (f32[64,1024]{1,0:T(8,128)S(1)}, f32[64,1024]{1,0:T(8,128)S(1)}, u32[]{:S(2)}, u32[]{:S(2)}) collective-permute-start(f32[64,1024]{1,0:T(8,128)S(1)} %add.1), channel_id=1, source_target_pairs={{0,2},{1,3},{2,0},{3,1},{4,6},{5,7},{6,4},{7,5},{8,10},{9,11},{10,... | collective-permute-start | bytes 786440 | tf_op jit(solution)/shard_map/ppermute | solution.py:81
  37.1 0.5 project_own.3.own_ref
  37.7 5.5 %collective-permute-done.61.across_ref = f32[64,1024]{1,0:T(8,128)S(1)} collective-permute-done((f32[64,1024]{1,0:T(8,128)S(1)}, f32[64,1024]{1,0:T(8,128)S(1)}, u32[]{:S(2)}, u32[]{:S(2)}) %collective-permute-start.61) | collective-permute-done | bytes 262176 | tf_op jit(solution)/shard_map/ppermute | solution.py:81
  43.2 10.1 %conditional.1 = (bf16[64,1024]{1,0:T(8,128)(2,1)}, bf16[64,1024]{1,0:T(8,128)(2,1)}) conditional(s32[]{:T(128)} %bitcast, bf16[64,1024]{1,0:T(8,128)(2,1)S(1)} %sum.1, bf16[64,1024]{1,0:T(8,128)(2,1)S(1)} %sum.1, bf16[64,1024]{1,0:T(8,128)(2,1)S(1)} %sum.1, bf16[64,1024]{1,0:T(8,128)(2,1)S(1)} %sum.1, ...), branch_computations={%region_0.0_spmd, %region_1.0_spmd, %region_2.0_spmd, %region_3.0_... | conditional | bytes 1048672 | solution.py:458
  43.3 3.3 %collective-permute-start.8 = (bf16[64,1024]{1,0:T(8,128)(2,1)S(1)}, bf16[64,1024]{1,0:T(8,128)(2,1)}, u32[]{:S(2)}, u32[]{:S(2)}) collective-permute-start(bf16[64,1024]{1,0:T(8,128)(2,1)S(1)} %param.4), channel_id=1, source_target_pairs={{0,2},{1,3},{2,0},{3,1},{12,6},{13,7},{14,4},{15,5},{4,10},{5,11},... | collective-permute-start | bytes 393224 | tf_op jit(solution)/shard_map/cond/branch_4_fun/ppermute | solution.py:451
  46.6 1.9 %collective-permute-start.7 = (bf16[64,1024]{1,0:T(8,128)(2,1)S(1)}, bf16[64,1024]{1,0:T(8,128)(2,1)}, u32[]{:S(2)}, u32[]{:S(2)}) collective-permute-start(bf16[64,1024]{1,0:T(8,128)(2,1)S(1)} %param.4), channel_id=1, source_target_pairs={{0,0},{1,1},{2,2},{3,3},{12,4},{13,5},{14,6},{15,7},{4,8},{5,9},{6... | collective-permute-start | bytes 393224 | tf_op jit(solution)/shard_map/cond/branch_4_fun/ppermute | solution.py:454
  48.6 0.5 collective-permute-done.8
  49.0 4.3 %collective-permute-done.7 = bf16[64,1024]{1,0:T(8,128)(2,1)} collective-permute-done((bf16[64,1024]{1,0:T(8,128)(2,1)S(1)}, bf16[64,1024]{1,0:T(8,128)(2,1)}, u32[]{:S(2)}, u32[]{:S(2)}) %collective-permute-start.7) | collective-permute-done | bytes 131104 | tf_op jit(solution)/shard_map/cond/branch_4_fun/ppermute | solution.py:454
  53.3 2.4 %collective-permute-start.62 = (bf16[64,1024]{1,0:T(8,128)(2,1)}, bf16[64,1024]{1,0:T(8,128)(2,1)S(1)}, u32[]{:S(2)}, u32[]{:S(2)}) collective-permute-start(bf16[64,1024]{1,0:T(8,128)(2,1)} %get-tuple-element.103.refs_0_), channel_id=1, source_target_pairs={{0,1},{1,0},{2,3},{3,2},{4,5},{5,4},{6,7},{7,6},{8,9},{9,8},{10,11... | collective-permute-start | bytes 393224 | tf_op jit(solution)/shard_map/ppermute | solution.py:81
  55.7 0.0 collective-permute-start.63
  55.7 1.7 %join.2.refs_2_ = bf16[1,64,4096]{2,1,0:T(8,128)(2,1)} custom-call(bf16[64,1024]{1,0:T(8,128)(2,1)} %get-tuple-element.103.refs_0_, bf16[64,1024]{1,0:T(8,128)(2,1)} %get-tuple-element.104.refs_1_), custom_call_target="tpu_custom_call" | custom-call | tf_op jit(solution)/shard_map/join/pallas_call | solution.py:322
  57.4 0.7 %join.3 = bf16[1,64,4096]{2,1,0:T(8,128)(2,1)} custom-call(bf16[64,1024]{1,0:T(8,128)(2,1)S(1)} %collective-permute-done.62.refs_0_, bf16[64,1024]{1,0:T(8,128)(2,1)S(1)} %collective-permute-done.63.refs_1_, bf16[1,64,4096]{2,1,0:T(8,128)(2,1)} %join.2.refs_2_), custom_call_target="tpu_custom_call", output_to_operand_aliasing={{}: (2, {})} | custom-call | tf_op jit(solution)/shard_map/join/pallas_call | solution.py:322
  (10 shorter events, 0.1 us)
Async XLA Ops:
  3.8 11.6 %collective-permute-start.48 = (bf16[384,512]{1,0:T(8,128)(2,1)S(1)}, bf16[384,512]{1,0:T(8,128)(2,1)S(1)}, u32[]{:S(2)}, u32[]{:S(2)}) collective-permute-start(bf16[384,512]{1,0:T(8,128)(2,1)S(1)} %get-tuple-element.76.refs_1_), channel_id=1, source_target_pairs={{0,2},{1,3},{2,0},{3,1},{4,6},{5,7},{6,4},{7,5},{8,10},{9,11},{10,... | collective-permute-start | bytes 1179656 | tf_op jit(solution)/shard_map/ppermute | solution.py:81
  5.1 10.3 %collective-permute-start.47 = (bf16[384,512]{1,0:T(8,128)(2,1)S(1)}, bf16[384,512]{1,0:T(8,128)(2,1)S(1)}, u32[]{:S(2)}, u32[]{:S(2)}) collective-permute-start(bf16[384,512]{1,0:T(8,128)(2,1)S(1)} %get-tuple-element.76.refs_1_), channel_id=1, source_target_pairs={{0,16},{16,0},{1,17},{17,1},{2,18},{18,2},{3,19},{19,3},{4,20},{20... | collective-permute-start | bytes 1179656 | tf_op jit(solution)/shard_map/ppermute | solution.py:81
  6.3 15.4 %copy-start = (bf16[2,512,256]{2,1,0:T(8,128)(2,1)S(1)}, bf16[2,512,256]{2,1,0:T(8,128)(2,1)}, u32[]{:S(2)}) copy-start(bf16[2,512,256]{2,1,0:T(8,128)(2,1)} %refs_4_.5) | copy-start | bytes 1572868
  6.3 8.3 %collective-permute-start.49 = (bf16[512,128]{1,0:T(8,128)(2,1)S(1)}, bf16[512,128]{1,0:T(8,128)(2,1)S(1)}, u32[]{:S(2)}, u32[]{:S(2)}) collective-permute-start(bf16[512,128]{1,0:T(8,128)(2,1)S(1)} %get-tuple-element.70.own_ref.refs_5_), channel_id=1, source_target_pairs={{0,8},{4,12},{8,0},{12,4},{1,9},{5,13},{9,1},{13,5},{2,10},{6,14},... | collective-permute-start | bytes 393224 | tf_op jit(solution)/shard_map/ppermute | solution.py:81
  15.2 3.9 %collective-permute-start.50 = (bf16[512,128]{1,0:T(8,128)(2,1)S(1)}, bf16[512,128]{1,0:T(8,128)(2,1)S(1)}, u32[]{:S(2)}, u32[]{:S(2)}) collective-permute-start(bf16[512,128]{1,0:T(8,128)(2,1)S(1)} %pass.1), channel_id=1, source_target_pairs={{0,4},{4,0},{8,12},{12,8},{1,5},{5,1},{9,13},{13,9},{2,6},{6,2},{1... | collective-permute-start | bytes 393224 | tf_op jit(solution)/shard_map/ppermute | solution.py:81
  15.4 7.9 %collective-permute-start.51 = (bf16[192,512]{1,0:T(8,128)(2,1)S(1)}, bf16[192,512]{1,0:T(8,128)(2,1)S(1)}, u32[]{:S(2)}, u32[]{:S(2)}) collective-permute-start(bf16[192,512]{1,0:T(8,128)(2,1)S(1)} %get-tuple-element.75), channel_id=1, source_target_pairs={{0,2},{1,3},{2,0},{3,1},{4,6},{5,7},{6,4},{7,5},{8,10},{9,11},{10,... | collective-permute-start | bytes 589832 | tf_op jit(solution)/shard_map/ppermute | solution.py:81
  15.7 7.5 %collective-permute-start.52 = (bf16[192,512]{1,0:T(8,128)(2,1)S(1)}, bf16[192,512]{1,0:T(8,128)(2,1)S(1)}, u32[]{:S(2)}, u32[]{:S(2)}) collective-permute-start(bf16[192,512]{1,0:T(8,128)(2,1)S(1)} %get-tuple-element.81), channel_id=1, source_target_pairs={{0,16},{16,0},{1,17},{17,1},{2,18},{18,2},{3,19},{19,3},{4,20},{20... | collective-permute-start | bytes 589832 | tf_op jit(solution)/shard_map/ppermute | solution.py:81
  16.4 7.5 %collective-permute-start.53 = (bf16[384,512]{1,0:T(8,128)(2,1)S(1)}, bf16[384,512]{1,0:T(8,128)(2,1)S(1)}, u32[]{:S(2)}, u32[]{:S(2)}) collective-permute-start(bf16[384,512]{1,0:T(8,128)(2,1)S(1)} %get-tuple-element.76.refs_1_), channel_id=1, source_target_pairs={{0,1},{1,0},{2,3},{3,2},{4,5},{5,4},{6,7},{7,6},{8,9},{9,8},{10,11... | collective-permute-start | bytes 1179656 | tf_op jit(solution)/shard_map/ppermute | solution.py:81
  18.7 5.1 %collective-permute-start.54 = (bf16[384,512]{1,0:T(8,128)(2,1)S(1)}, bf16[384,512]{1,0:T(8,128)(2,1)S(1)}, u32[]{:S(2)}, u32[]{:S(2)}) collective-permute-start(bf16[384,512]{1,0:T(8,128)(2,1)S(1)} %collective-permute-done.47.near_ref.refs_2_), channel_id=1, source_target_pairs={{0,1},{1,0},{2,3},{3,2},{4,5},{5,4},{6,7},{7,6},{8,9},{9,8},{10,11... | collective-permute-start | bytes 1179656 | tf_op jit(solution)/shard_map/ppermute | solution.py:81
  19.0 4.8 %collective-permute-start.55 = (bf16[384,512]{1,0:T(8,128)(2,1)S(1)}, bf16[384,512]{1,0:T(8,128)(2,1)S(1)}, u32[]{:S(2)}, u32[]{:S(2)}) collective-permute-start(bf16[384,512]{1,0:T(8,128)(2,1)S(1)} %collective-permute-done.48.far_ref.refs_3_), channel_id=1, source_target_pairs={{0,1},{1,0},{2,3},{3,2},{4,5},{5,4},{6,7},{7,6},{8,9},{9,8},{10,11... | collective-permute-start | bytes 1179656 | tf_op jit(solution)/shard_map/ppermute | solution.py:81
  23.3 1.6 %collective-permute-start.56 = (bf16[192,512]{1,0:T(8,128)(2,1)S(1)}, bf16[192,512]{1,0:T(8,128)(2,1)S(1)}, u32[]{:S(2)}, u32[]{:S(2)}) collective-permute-start(bf16[192,512]{1,0:T(8,128)(2,1)S(1)} %collective-permute-done.51.refs_0_), channel_id=1, source_target_pairs={{0,1},{1,0},{2,3},{3,2},{4,5},{5,4},{6,7},{7,6},{8,9},{9,8},{10,11... | collective-permute-start | bytes 589832 | tf_op jit(solution)/shard_map/ppermute | solution.py:81
  23.5 1.6 %collective-permute-start.57 = (bf16[192,512]{1,0:T(8,128)(2,1)S(1)}, bf16[192,512]{1,0:T(8,128)(2,1)S(1)}, u32[]{:S(2)}, u32[]{:S(2)}) collective-permute-start(bf16[192,512]{1,0:T(8,128)(2,1)S(1)} %collective-permute-done.52.refs_1_), channel_id=1, source_target_pairs={{0,1},{1,0},{2,3},{3,2},{4,5},{5,4},{6,7},{7,6},{8,9},{9,8},{10,11... | collective-permute-start | bytes 589832 | tf_op jit(solution)/shard_map/ppermute | solution.py:81
  27.3 4.9 %collective-permute-start.58 = (bf16[64,1024]{1,0:T(8,128)(2,1)S(1)}, bf16[64,1024]{1,0:T(8,128)(2,1)S(1)}, u32[]{:S(2)}, u32[]{:S(2)}) collective-permute-start(bf16[64,1024]{1,0:T(8,128)(2,1)S(1)} %attend.1.refs_0_), channel_id=1, source_target_pairs={{0,16},{16,0},{1,17},{17,1},{2,18},{18,2},{3,19},{19,3},{4,20},{20... | collective-permute-start | bytes 393224 | tf_op jit(solution)/shard_map/ppermute | solution.py:81
  32.7 2.3 %collective-permute-start.59 = (f32[64,1024]{1,0:T(8,128)S(1)}, f32[64,1024]{1,0:T(8,128)S(1)}, u32[]{:S(2)}, u32[]{:S(2)}) collective-permute-start(f32[64,1024]{1,0:T(8,128)S(1)} %project_sent.2), channel_id=1, source_target_pairs={{0,1},{1,0},{2,3},{3,2},{4,5},{5,4},{6,7},{7,6},{8,9},{9,8},{10,11... | collective-permute-start | bytes 786440 | tf_op jit(solution)/shard_map/ppermute | solution.py:81
  35.0 2.7 %collective-permute-start.60 = (f32[64,1024]{1,0:T(8,128)S(1)}, f32[64,1024]{1,0:T(8,128)S(1)}, u32[]{:S(2)}, u32[]{:S(2)}) collective-permute-start(f32[64,1024]{1,0:T(8,128)S(1)} %project_sent.3), channel_id=1, source_target_pairs={{0,1},{1,0},{2,3},{3,2},{4,5},{5,4},{6,7},{7,6},{8,9},{9,8},{10,11... | collective-permute-start | bytes 786440 | tf_op jit(solution)/shard_map/ppermute | solution.py:81
  35.4 7.8 %collective-permute-start.61 = (f32[64,1024]{1,0:T(8,128)S(1)}, f32[64,1024]{1,0:T(8,128)S(1)}, u32[]{:S(2)}, u32[]{:S(2)}) collective-permute-start(f32[64,1024]{1,0:T(8,128)S(1)} %add.1), channel_id=1, source_target_pairs={{0,2},{1,3},{2,0},{3,1},{4,6},{5,7},{6,4},{7,5},{8,10},{9,11},{10,... | collective-permute-start | bytes 786440 | tf_op jit(solution)/shard_map/ppermute | solution.py:81
  43.3 5.8 %collective-permute-start.8 = (bf16[64,1024]{1,0:T(8,128)(2,1)S(1)}, bf16[64,1024]{1,0:T(8,128)(2,1)}, u32[]{:S(2)}, u32[]{:S(2)}) collective-permute-start(bf16[64,1024]{1,0:T(8,128)(2,1)S(1)} %param.4), channel_id=1, source_target_pairs={{0,2},{1,3},{2,0},{3,1},{12,6},{13,7},{14,4},{15,5},{4,10},{5,11},... | collective-permute-start | bytes 393224 | tf_op jit(solution)/shard_map/cond/branch_4_fun/ppermute | solution.py:451
  46.6 6.7 %collective-permute-start.7 = (bf16[64,1024]{1,0:T(8,128)(2,1)S(1)}, bf16[64,1024]{1,0:T(8,128)(2,1)}, u32[]{:S(2)}, u32[]{:S(2)}) collective-permute-start(bf16[64,1024]{1,0:T(8,128)(2,1)S(1)} %param.4), channel_id=1, source_target_pairs={{0,0},{1,1},{2,2},{3,3},{12,4},{13,5},{14,6},{15,7},{4,8},{5,9},{6... | collective-permute-start | bytes 393224 | tf_op jit(solution)/shard_map/cond/branch_4_fun/ppermute | solution.py:454
  53.3 4.1 %collective-permute-start.62 = (bf16[64,1024]{1,0:T(8,128)(2,1)}, bf16[64,1024]{1,0:T(8,128)(2,1)S(1)}, u32[]{:S(2)}, u32[]{:S(2)}) collective-permute-start(bf16[64,1024]{1,0:T(8,128)(2,1)} %get-tuple-element.103.refs_0_), channel_id=1, source_target_pairs={{0,1},{1,0},{2,3},{3,2},{4,5},{5,4},{6,7},{7,6},{8,9},{9,8},{10,11... | collective-permute-start | bytes 393224 | tf_op jit(solution)/shard_map/ppermute | solution.py:81
  55.7 1.7 %collective-permute-start.63 = (bf16[64,1024]{1,0:T(8,128)(2,1)}, bf16[64,1024]{1,0:T(8,128)(2,1)S(1)}, u32[]{:S(2)}, u32[]{:S(2)}) collective-permute-start(bf16[64,1024]{1,0:T(8,128)(2,1)} %get-tuple-element.104.refs_1_), channel_id=1, source_target_pairs={{0,1},{1,0},{2,3},{3,2},{4,5},{5,4},{6,7},{7,6},{8,9},{9,8},{10,11... | collective-permute-start | bytes 393224 | tf_op jit(solution)/shard_map/ppermute | solution.py:81
